TPU v7x, 32 devices: a whole 2x2x4 slice. The times are simulated.
32 devices in a mesh: obs: 4 (over y, x), unk: 8 (over z, core).
Axes of the slice: x: 2, y: 2, z: 4, core: 2. Of those that a mesh axis runs over, the one named last changes fastest.
Arguments:
- design: float32 [4096, 24576], P('obs', 'unk'), may hold values from -0.09375 to 0.09375
- weights: float32 [4096], P('obs'), may hold values from 0.25 to 4
Outputs:
- factor: float32 [24576, 1024], P(('unk', 'obs'))
All inputs are finite; a program needn't handle non-finite values.
Results may differ from a plain program's by a relative error of at most 0.00011.
Values sent between devices are 32-bit elements; how exact they have to be, the bound alone decides.
A program may use at most 128 MiB of HBM per device.

v0:
```python
import jax
import jax.numpy as jnp
from jax import lax
from jax.sharding import PartitionSpec as P

PANEL = 512
BLOCK = 128


def spread(block, axis, holder):
    block = jnp.where(lax.axis_index(axis) == holder, block, jnp.zeros_like(block))
    return lax.psum(block, axis)


def apply_lower(diag_factor, values):
    return lax.linalg.triangular_solve(
        diag_factor, values, left_side=False, lower=True, transpose_a=True
    )


def left_looking(top_block, owned_rows):
    width = top_block.shape[0]
    factor_top = jnp.zeros_like(top_block)
    factor_rows = jnp.zeros_like(owned_rows)
    for column_block in range(width // BLOCK):
        offset = column_block * BLOCK
        update_top = top_block[:, offset : offset + BLOCK]
        update_rows = owned_rows[:, offset : offset + BLOCK]
        if offset > 0:
            earlier = factor_top[offset : offset + BLOCK, :offset]
            update_top = update_top - jnp.dot(
                factor_top[:, :offset],
                earlier.T,
                precision=lax.Precision.HIGHEST,
                preferred_element_type=jnp.float32,
            )
            update_rows = update_rows - jnp.dot(
                factor_rows[:, :offset],
                earlier.T,
                precision=lax.Precision.HIGHEST,
                preferred_element_type=jnp.float32,
            )
        diag_factor = jnp.linalg.cholesky(update_top[offset : offset + BLOCK])
        below_top = apply_lower(diag_factor, update_top[offset + BLOCK :])
        new_column = jnp.concatenate(
            [jnp.zeros((offset, BLOCK), jnp.float32), diag_factor, below_top], axis=0
        )
        factor_top = factor_top.at[:, offset : offset + BLOCK].set(new_column)
        factor_rows = factor_rows.at[:, offset : offset + BLOCK].set(
            apply_lower(diag_factor, update_rows)
        )
    return factor_rows


def local(design, weights):
    panel_cols = spread(design[:, : 2 * PANEL], "unk", 0)
    weighted = panel_cols * weights[:, None]
    partial_value = lax.dot_general(
        design,
        weighted,
        (((0,), (0,)), ((), ())),
        precision=lax.Precision.HIGHEST,
        preferred_element_type=jnp.float32,
    )
    owned_rows = lax.psum_scatter(partial_value, "obs", scatter_dimension=0, tiled=True)
    local_top = lax.dot_general(
        panel_cols,
        weighted,
        (((0,), (0,)), ((), ())),
        precision=lax.Precision.HIGHEST,
        preferred_element_type=jnp.float32,
    )
    top_block = lax.psum(local_top, "obs")
    return left_looking(top_block, owned_rows)


def solution(mesh):
    return jax.shard_map(
        local,
        mesh=mesh,
        in_specs=(P("obs", "unk"), P("obs")),
        out_specs=P(("unk", "obs"), None),
        check_vma=False,
    )
```

profile of v0, /device:TPU:25, one launch (start us, length us, event | category | flops | bytes accessed | tf_op | source)
XLA Modules:
  0.0 549.0 jit_solution(5342032945112979178)
XLA Ops:
  6.5 4.9 slice_select_fusion
  11.6 96.8 %all-reduce.5.cloned.1.call-done = f32[1024,1024]{1,0:T(8,128)} async-done(((f32[1024,1024]{1,0:T(8,128)}), f32[1024,1024]{1,0:T(8,128)}) %all-reduce.5.cloned.1.call-update) | async-done | bytes 4194320 | tf_op jit(solution)/shard_map/psum | solution.py:12
  108.4 18.1 %fusion.1 = f32[1024,1024]{0,1:T(8,128)} fusion(f32[1024,1024]{1,0:T(8,128)} %all-reduce.5.cloned.1.call-done, f32[1024]{0:T(1024)S(1)} %copy-done.16), kind=kOutput, calls=%fused_computation.2 | convolution fusion | flops 12885950464 | bytes 8392704 | tf_op jit(solution)/shard_map/dot_general | solution.py:66
  127.1 47.5 %convolution_bitcast_fusion = f32[3072,1024]{0,1:T(8,128)} fusion(f32[1024,3072]{1,0:T(8,128)} %param.35, f32[1024,1024]{1,0:T(8,128)} %all-reduce.5.cloned.1.call-done, f32[1024]{0:T(1024)S(1)} %copy-done.16), kind=kOutput, calls=%fused_computation | convolution fusion | flops 38655754240 | bytes 29364224 | tf_op jit(solution)/shard_map/dot_general | solution.py:58
  179.6 51.7 %all-reduce.7.cloned.1.call-done = f32[1024,1024]{0,1:T(8,128)} async-done(((f32[1024,1024]{0,1:T(8,128)}), f32[1024,1024]{0,1:T(8,128)}) %all-reduce.7.cloned.1.call-update) | async-done | bytes 4194320 | tf_op jit(solution)/shard_map/psum | solution.py:73
  233.1 11.7 %cholesky.134 = f32[128,128]{1,0:T(8,128)S(1)} custom-call(f32[128,128]{1,0:T(8,128)S(1)} %fusion.119), custom_call_target="Cholesky" | custom-call | tf_op jit(solution)/shard_map/jit(cholesky)/cholesky | solution.py:43
  246.2 9.8 %custom-call.37 = f32[1,128,128]{1,2,0:T(8,128)S(1)} custom-call(f32[1,128,128]{2,1,0:T(8,128)S(1)} %get-tuple-element.199), custom_call_target="InvertDiagBlocksLowerTriangular" | custom-call | tf_op jit(solution)/shard_map/triangular_solve/custom-call.0 | solution.py:16
  261.7 11.7 %cholesky.145 = f32[128,128]{1,0:T(8,128)S(1)} custom-call(f32[128,128]{1,0:T(8,128)S(1)} %fusion.116), custom_call_target="Cholesky" | custom-call | tf_op jit(solution)/shard_map/jit(cholesky)/cholesky | solution.py:43
  274.7 10.0 %custom-call.38 = f32[1,128,128]{1,2,0:T(8,128)S(1)} custom-call(f32[1,128,128]{2,1,0:T(8,128)S(1)} %get-tuple-element.197), custom_call_target="InvertDiagBlocksLowerTriangular" | custom-call | tf_op jit(solution)/shard_map/triangular_solve/custom-call.0 | solution.py:16
  289.2 11.7 %cholesky.156 = f32[128,128]{1,0:T(8,128)S(1)} custom-call(f32[128,128]{1,0:T(8,128)S(1)} %fusion.113), custom_call_target="Cholesky" | custom-call | tf_op jit(solution)/shard_map/jit(cholesky)/cholesky | solution.py:43
  302.2 9.8 %custom-call.40 = f32[1,128,128]{1,2,0:T(8,128)S(1)} custom-call(f32[1,128,128]{2,1,0:T(8,128)S(1)} %get-tuple-element.195), custom_call_target="InvertDiagBlocksLowerTriangular" | custom-call | tf_op jit(solution)/shard_map/triangular_solve/custom-call.0 | solution.py:16
  313.2 42.3 %reduce-scatter.2.cloned.1.call-done = f32[768,1024]{0,1:T(8,128)} async-done(((f32[3072,1024]{0,1:T(8,128)}), f32[768,1024]{0,1:T(8,128)}) %reduce-scatter.2.cloned.1.call-update) | async-done | bytes 3145744 | tf_op jit(solution)/shard_map/reduce_scatter | solution.py:65
  364.1 2.6 fusion.68
  366.7 2.6 fusion.26
  371.1 11.7 %cholesky.167 = f32[128,128]{1,0:T(8,128)S(1)} custom-call(f32[128,128]{1,0:T(8,128)S(1)} %fusion.110), custom_call_target="Cholesky" | custom-call | tf_op jit(solution)/shard_map/jit(cholesky)/cholesky | solution.py:43
  384.7 9.8 %custom-call.41 = f32[1,128,128]{1,2,0:T(8,128)S(1)} custom-call(f32[1,128,128]{2,1,0:T(8,128)S(1)} %get-tuple-element.193), custom_call_target="InvertDiagBlocksLowerTriangular" | custom-call | tf_op jit(solution)/shard_map/triangular_solve/custom-call.0 | solution.py:16
  400.3 2.6 fusion.67
  402.9 2.9 fusion.32
  407.6 11.9 %cholesky.178 = f32[128,128]{1,0:T(8,128)S(1)} custom-call(f32[128,128]{1,0:T(8,128)S(1)} %fusion.107), custom_call_target="Cholesky" | custom-call | tf_op jit(solution)/shard_map/jit(cholesky)/cholesky | solution.py:43
  420.8 9.8 %custom-call.42 = f32[1,128,128]{1,2,0:T(8,128)S(1)} custom-call(f32[1,128,128]{2,1,0:T(8,128)S(1)} %get-tuple-element.191), custom_call_target="InvertDiagBlocksLowerTriangular" | custom-call | tf_op jit(solution)/shard_map/triangular_solve/custom-call.0 | solution.py:16
  435.6 2.5 fusion.66
  438.1 3.5 fusion.29
  443.4 11.9 %cholesky.189 = f32[128,128]{1,0:T(8,128)S(1)} custom-call(f32[128,128]{1,0:T(8,128)S(1)} %fusion.104), custom_call_target="Cholesky" | custom-call | tf_op jit(solution)/shard_map/jit(cholesky)/cholesky | solution.py:43
  456.6 9.8 %custom-call.43 = f32[1,128,128]{1,2,0:T(8,128)S(1)} custom-call(f32[1,128,128]{2,1,0:T(8,128)S(1)} %get-tuple-element.189), custom_call_target="InvertDiagBlocksLowerTriangular" | custom-call | tf_op jit(solution)/shard_map/triangular_solve/custom-call.0 | solution.py:16
  467.7 2.7 fusion.35
  474.4 3.1 fusion.23
  479.3 11.7 %cholesky.200 = f32[128,128]{1,0:T(8,128)S(1)} custom-call(f32[128,128]{1,0:T(8,128)S(1)} %fusion.101), custom_call_target="Cholesky" | custom-call | tf_op jit(solution)/shard_map/jit(cholesky)/cholesky | solution.py:43
  492.3 10.2 %custom-call.44 = f32[1,128,128]{1,2,0:T(8,128)S(1)} custom-call(f32[1,128,128]{2,1,0:T(8,128)S(1)} %get-tuple-element.187), custom_call_target="InvertDiagBlocksLowerTriangular" | custom-call | tf_op jit(solution)/shard_map/triangular_solve/custom-call.0 | solution.py:16
  503.7 2.8 fusion.55
  513.3 11.7 %cholesky.211 = f32[128,128]{1,0:T(8,128)S(1)} custom-call(f32[128,128]{1,0:T(8,128)S(1)} %fusion.98), custom_call_target="Cholesky" | custom-call | tf_op jit(solution)/shard_map/jit(cholesky)/cholesky | solution.py:43
  526.4 10.0 %custom-call.45 = f32[1,128,128]{1,2,0:T(8,128)S(1)} custom-call(f32[1,128,128]{2,1,0:T(8,128)S(1)} %fusion.94), custom_call_target="InvertDiagBlocksLowerTriangular" | custom-call | tf_op jit(solution)/shard_map/triangular_solve/custom-call.0 | solution.py:16
  536.3 3.1 fusion.38
  (144 shorter events, 71.9 us)
Async XLA Ops:
  6.5 101.8 %all-reduce.5.cloned.1.call-start = ((), (), s32[]{:S(2)}) async-start(), calls=%async_computation.1 | async-start | bytes 8388608 | tf_op jit(solution)/shard_map/psum | solution.py:12
  11.5 96.9 %copy-start.16 = (f32[1024]{0:T(1024)S(1)}, f32[1024]{0:T(1024)}, u32[]{:S(2)}) copy-start(f32[1024]{0:T(1024)} %param.36) | copy-start | bytes 12292
  11.5 219.8 %all-reduce.7.cloned.1.call-start = ((), (), s32[]{:S(2)}) async-start(), calls=%async_computation.2 | async-start | bytes 8388608 | tf_op jit(solution)/shard_map/psum | solution.py:73
  126.5 229.1 %reduce-scatter.2.cloned.1.call-start = ((), (), s32[]{:S(2)}) async-start(), calls=%async_computation.3 | async-start | bytes 15728640 | tf_op jit(solution)/shard_map/reduce_scatter | solution.py:65
  256.1 4.8 copy-start.5
  258.5 2.5 copy-start.4
  312.0 43.5 %copy-start.13 = (f32[1,128,128]{1,2,0:T(8,128)}, f32[1,128,128]{1,2,0:T(8,128)S(1)}, u32[]{:S(2)}) copy-start(f32[1,128,128]{1,2,0:T(8,128)S(1)} %custom-call.40) | copy-start | bytes 196612
  357.6 4.7 copy-start.14
  357.6 6.4 %copy-start.15 = (f32[128,128]{0,1:T(8,128)S(1)}, f32[128,128]{0,1:T(8,128)}, u32[]{:S(2)}) copy-start(f32[128,128]{0,1:T(8,128)} %copy.13) | copy-start | bytes 196612
  357.6 9.1 %copy-start.6 = (f32[1024,1024]{0,1:T(8,128)S(1)}, f32[1024,1024]{0,1:T(8,128)}, u32[]{:S(2)}) copy-start(f32[1024,1024]{0,1:T(8,128)} %all-reduce.7.cloned.1.call-done) | copy-start | bytes 12582916
  369.3 0.8 copy-start.9
  396.8 6.2 %copy-start.7 = (f32[1024,1024]{0,1:T(8,128)S(1)}, f32[1024,1024]{0,1:T(8,128)}, u32[]{:S(2)}) copy-start(f32[1024,1024]{0,1:T(8,128)} %all-reduce.7.cloned.1.call-done) | copy-start | bytes 12582916
  405.9 0.8 copy-start.10
  432.0 6.1 %copy-start.8 = (f32[1024,1024]{0,1:T(8,128)S(1)}, f32[1024,1024]{0,1:T(8,128)}, u32[]{:S(2)}) copy-start(f32[1024,1024]{0,1:T(8,128)} %all-reduce.7.cloned.1.call-done) | copy-start | bytes 12582916
  441.6 0.8 copy-start.11
  467.7 4.0 copy-start
  472.5 1.9 copy-start.1
  477.5 0.8 copy-start.12
  503.7 4.3 copy-start.2
  506.5 6.6 %slice-start = ((f32[1024,1024]{0,1:T(8,128)}), f32[1024,128]{0,1:T(8,128)S(1)}, s32[]{:S(2)}) async-start(f32[1024,1024]{0,1:T(8,128)} %all-reduce.7.cloned.1.call-done), calls=%async_computation.4 | async-start | bytes 1048576 | tf_op jit(solution)/shard_map/slice | solution.py:27
  508.8 1.9 copy-start.3
Sparse Core Ops, SparseCore 0:
  11.6 96.7 all-reduce.4
  126.6 104.6 all-reduce.6
  234.7 120.7 reduce-scatter.1
where the time goes:
time: 558 us; the launch traced here: 549 us
  other arithmetic  210 us (38%)
  waiting for transfers between devices  191 us (34%)
  matrix products  118 us (21%)
  local copies, waits for them, and re-layouts  15.8 us (3%)
  between operations  14.1 us (3%)
    another operation x24, other arithmetic, left_looking(): diag_factor = jnp.linalg.cholesky(update_top[offset:offset + BLOCK])  99.5 us
    psum x1, waiting for transfers between devices, spread(): return lax.psum(block, axis)  96.8 us
    another operation x16, other arithmetic, apply_lower(): lax.linalg.triangular_solve(diag_factor, values, left_side=False, lower=T...  84.6 us
    psum x1, waiting for transfers between devices, local(): top_block = lax.psum(local_top, 'obs')  51.7 us
    dot_general x1, matrix products, local(): lax.dot_general(design, weighted, (((0,), (0,)), ((), ())), precision=lax...  47.5 us
    reduce_scatter x1, waiting for transfers between devices, local(): lax.psum_scatter(partial_value, 'obs', scatter_dimension=0, tiled=True)  42.3 us
    another operation x15, matrix products, apply_lower(): lax.linalg.triangular_solve(diag_factor, values, left_side=False, lower=T...  18.3 us
    dot_general x1, matrix products, local(): lax.dot_general(panel_cols, weighted, (((0,), (0,)), ((), ())), precision...  18.1 us
  transfers between devices with their start and end apart: 3, of which 3 were waited for; matrix products, arithmetic and copies ran while one was open for 24% of the time, Pallas kernels for 0%

commit v1 on v0

v1 whole, which is shorter than its diff:
```python
import functools
import jax
import jax.numpy as jnp
from jax import lax
from jax.experimental import pallas as pl
from jax.experimental.pallas import tpu as pltpu
from jax.sharding import PartitionSpec as P

PANEL = 512
BLOCK = 128
STRIP = 8


def split(value):
    high = value.astype(jnp.bfloat16)
    low = (value - high.astype(jnp.float32)).astype(jnp.bfloat16)
    return high, low


def dot_t(left, right):
    return lax.dot_general(
        left, right, (((0,), (0,)), ((), ())), preferred_element_type=jnp.float32
    )


def dot_3(left, right):
    left_high, left_low = split(left)
    right_high, right_low = split(right)
    dot = functools.partial(jnp.dot, preferred_element_type=jnp.float32)
    return dot(left_high, right_high) + dot(left_high, right_low) + dot(left_low, right_high)


def invert_factor(work):
    row = lax.broadcasted_iota(jnp.int32, (STRIP, 2 * BLOCK), 0)
    for strip in range(BLOCK // STRIP):
        start = strip * STRIP
        rows = work[start : start + STRIP, :]
        scale = jnp.zeros_like(rows)
        for step in range(STRIP):
            column = jnp.broadcast_to(
                rows[:, start + step : start + step + 1], (STRIP, 2 * BLOCK)
            )
            pivot = jnp.broadcast_to(column[step : step + 1, :], (STRIP, 2 * BLOCK))
            scale = jnp.where(row == step, pivot, scale)
            if step < STRIP - 1:
                pivot_row = jnp.broadcast_to(rows[step : step + 1, :], (STRIP, 2 * BLOCK))
                factor = jnp.where(row > step, column / pivot, 0.0)
                rows = rows - factor * pivot_row
        rows = rows * lax.rsqrt(scale)
        work[start : start + STRIP, :] = rows
        if start + STRIP < BLOCK:
            first = rows.astype(jnp.bfloat16).astype(jnp.float32)
            rest = rows - first
            second = rest.astype(jnp.bfloat16).astype(jnp.float32)
            third = rest - second
            right = jnp.concatenate([first, second, first, second, third, first], axis=0)
            left = jnp.concatenate([first, first, second, second, first, third], axis=0)
            update = dot_t(
                left[:, :BLOCK].astype(jnp.bfloat16), right.astype(jnp.bfloat16)
            )
            work[start + STRIP :, :] = work[start + STRIP :, :] - update[start + STRIP :, :]


def factor_kernel(both_ref, out_ref, done, work, block):
    width, total = both_ref.shape
    eye = (
        lax.broadcasted_iota(jnp.int32, (BLOCK, BLOCK), 0)
        == lax.broadcasted_iota(jnp.int32, (BLOCK, BLOCK), 1)
    ).astype(jnp.float32)

    def step(k, _):
        offset = pl.multiple_of(k * BLOCK, BLOCK)
        block[...] = both_ref[pl.ds(offset, BLOCK), :]

        def earlier(j, _):
            held = done[j, :, pl.ds(offset, BLOCK)]
            left = jnp.concatenate(
                [held[:BLOCK], held[2 * BLOCK :], held[BLOCK : 2 * BLOCK]], axis=0
            )
            block[...] = block[...] - dot_t(left, done[j])
            return 0

        lax.fori_loop(0, k, earlier, 0)
        work[:, :BLOCK] = block[:, pl.ds(offset, BLOCK)]
        work[:, BLOCK:] = eye
        invert_factor(work)
        column = dot_3(work[:, BLOCK:], block[...])
        high, low = split(column)
        done[k, :BLOCK, :] = high
        done[k, BLOCK : 2 * BLOCK, :] = low
        done[k, 2 * BLOCK :, :] = high
        out_ref[pl.ds(offset, BLOCK), :] = column[:, width:]
        return 0

    lax.fori_loop(0, width // BLOCK, step, 0)


def factor_rows(both):
    width, total = both.shape
    return pl.pallas_call(
        factor_kernel,
        out_shape=jax.ShapeDtypeStruct((width, total - width), jnp.float32),
        in_specs=[pl.BlockSpec(memory_space=pltpu.VMEM)],
        out_specs=pl.BlockSpec(memory_space=pltpu.VMEM),
        scratch_shapes=[
            pltpu.VMEM((width // BLOCK, 3 * BLOCK, total), jnp.bfloat16),
            pltpu.VMEM((BLOCK, 2 * BLOCK), jnp.float32),
            pltpu.VMEM((BLOCK, total), jnp.float32),
        ],
        compiler_params=pltpu.CompilerParams(vmem_limit_bytes=56 * 2**20),
    )(both)


def spread(block, axis, holder):
    block = jnp.where(lax.axis_index(axis) == holder, block, jnp.zeros_like(block))
    return lax.psum(block, axis)


def local(design, weights):
    panel_cols = spread(design[:, : 2 * PANEL], "unk", 0)
    weighted = panel_cols * weights[:, None]
    dot = functools.partial(
        lax.dot_general,
        dimension_numbers=(((0,), (0,)), ((), ())),
        precision=lax.Precision.HIGH,
        preferred_element_type=jnp.float32,
    )
    top_block = lax.psum(dot(weighted, panel_cols), "obs")
    partial_value = dot(weighted, design)
    owned = lax.psum_scatter(partial_value, "obs", scatter_dimension=1, tiled=True)
    return factor_rows(jnp.concatenate([top_block, owned], axis=1)).T


def solution(mesh):
    return jax.shard_map(
        local,
        mesh=mesh,
        in_specs=(P("obs", "unk"), P("obs")),
        out_specs=P(("unk", "obs"), None),
        check_vma=False,
    )
```

time: 558 us -> 526 us (0.943); the launches traced: 549 us -> 524 us
  other arithmetic: 210 us -> 11.6 us
  Pallas kernels: 0 us -> 158 us
  waiting for transfers between devices: 191 us -> 297 us
  matrix products: 118 us -> 40.4 us
  local copies, waits for them, and re-layouts: 15.8 us -> 3.54 us
    another operation x47 -> x0, other arithmetic: 189 us -> none  [the longest x24 99.5 us: left_looking(): diag_factor = jnp.linalg.cholesky(update_top[offset:offset + BLOCK])]
    pallas_call x0 -> x1, Pallas kernels: none -> 158 us  [factor_rows(): pl.pallas_call(factor_kernel, out_shape=jax.ShapeDtypeStruct((width, tota...]
    reduce_scatter x1, waiting for transfers between devices: 42.3 us -> 124 us  [local(): lax.psum_scatter(partial_value, 'obs', scatter_dimension=1, tiled=True)]
    dot_general x16 -> x2, matrix products: 99.5 us -> 40.4 us  [the longest x1 28.7 us: local(): partial_value = dot(weighted, design)]
    psum x1, waiting for transfers between devices: 51.7 us -> 75.9 us  [local(): top_block = lax.psum(dot(weighted, panel_cols), 'obs')]
    another operation x15 -> x0, matrix products: 18.3 us -> none  [apply_lower(): lax.linalg.triangular_solve(diag_factor, values, left_side=False, lower=T...]
    scatter x6 -> x0, other arithmetic: 10.8 us -> none  [left_looking(): factor_top = factor_top.at[:, offset:offset + BLOCK].set(new_column)]
    unnamed x34 -> x2, local copies, waits for them, and re-layouts: 7.04 us -> 0.01 us
  transfers between devices with their start and end apart: 3 -> 3, of which waited for: 3 -> 3; matrix products, arithmetic and copies ran while one was open for 24% -> 5% of each run, Pallas kernels for 0% -> 0%
where the time goes in v1:
time: 526 us; the launch traced here: 524 us
  waiting for transfers between devices  297 us (56%)
  Pallas kernels  158 us (30%)
  matrix products  40.4 us (8%)
  between operations  13.1 us (2%)
  other arithmetic  11.6 us (2%)
    pallas_call x1, Pallas kernels, factor_rows(): pl.pallas_call(factor_kernel, out_shape=jax.ShapeDtypeStruct((width, tota...  158 us
    reduce_scatter x1, waiting for transfers between devices, local(): lax.psum_scatter(partial_value, 'obs', scatter_dimension=1, tiled=True)  124 us
    psum x1, waiting for transfers between devices, spread(): return lax.psum(block, axis)  96.8 us
    psum x1, waiting for transfers between devices, local(): top_block = lax.psum(dot(weighted, panel_cols), 'obs')  75.9 us
    dot_general x1, matrix products, local(): partial_value = dot(weighted, design)  28.7 us
    dot_general x1, matrix products, local(): top_block = lax.psum(dot(weighted, panel_cols), 'obs')  11.7 us
  transfers between devices with their start and end apart: 3, of which 3 were waited for; matrix products, arithmetic and copies ran while one was open for 5% of the time, Pallas kernels for 0%

profile of v1, /device:TPU:25, one launch (start us, length us, event | category | flops | bytes accessed | tf_op | source)
XLA Modules:
  0.0 524.0 jit_solution(3099388730298912651)
XLA Ops:
  6.5 0.0 all-reduce.3.cloned.1.call-start
  6.5 4.9 slice_select_fusion
  11.5 0.0 copy-start
  11.5 0.0 all-reduce.3.cloned.1.call-update
  11.5 0.0 all-reduce.5.cloned.1.call-start
  11.6 96.8 %all-reduce.3.cloned.1.call-done = f32[1024,1024]{1,0:T(8,128)} async-done(((f32[1024,1024]{1,0:T(8,128)}), f32[1024,1024]{1,0:T(8,128)}) %all-reduce.3.cloned.1.call-update) | async-done | bytes 4194320 | tf_op jit(solution)/shard_map/psum | solution.py:116
  108.4 0.0 copy-done
  108.4 11.7 %fusion.2 = f32[1024,1024]{1,0:T(8,128)} fusion(f32[1024,1024]{1,0:T(8,128)} %all-reduce.3.cloned.1.call-done, f32[1024]{0:T(1024)S(1)} %copy-done), kind=kOutput, calls=%fused_computation.3 | convolution fusion | flops 6443499520 | bytes 8392704 | tf_op jit(solution)/shard_map/dot_general | solution.py:128
  120.1 0.0 all-reduce.5.cloned.1.call-update
  120.1 0.2 reduce-scatter.2.cloned.1.call-start
  120.4 28.7 %fusion = f32[1024,3072]{1,0:T(8,128)} fusion(f32[1024,3072]{1,0:T(8,128)} %param.2, f32[1024,1024]{1,0:T(8,128)} %all-reduce.3.cloned.1.call-done, f32[1024]{0:T(1024)S(1)} %copy-done), kind=kOutput, calls=%fused_computation.1 | convolution fusion | flops 19328401408 | bytes 29364224 | tf_op jit(solution)/shard_map/dot_general | solution.py:129
  149.1 0.0 reduce-scatter.2.cloned.1.call-update
  149.1 75.9 %all-reduce.5.cloned.1.call-done = f32[1024,1024]{1,0:T(8,128)} async-done(((f32[1024,1024]{1,0:T(8,128)}), f32[1024,1024]{1,0:T(8,128)}) %all-reduce.5.cloned.1.call-update) | async-done | bytes 4194320 | tf_op jit(solution)/shard_map/psum | solution.py:128
  225.0 124.2 %reduce-scatter.2.cloned.1.call-done = f32[1024,768]{1,0:T(8,128)} async-done(((f32[1024,3072]{1,0:T(8,128)}), f32[1024,768]{1,0:T(8,128)}) %reduce-scatter.2.cloned.1.call-update) | async-done | bytes 3145744 | tf_op jit(solution)/shard_map/reduce_scatter | solution.py:130
  349.2 6.7 %pad_maximum_fusion.both_ref = f32[1024,1792]{1,0:T(8,128)} fusion(f32[1024,768]{1,0:T(8,128)} %reduce-scatter.2.cloned.1.call-done, f32[1024,1024]{1,0:T(8,128)} %all-reduce.5.cloned.1.call-done), kind=kLoop, calls=%fused_computation | loop fusion | flops 1835008 | bytes 14680064 | tf_op jit(solution)/shard_map/concatenate | solution.py:131
  355.8 158.0 %shard_map.28 = f32[1024,768]{1,0:T(8,128)} custom-call(f32[1024,1792]{1,0:T(8,128)} %pad_maximum_fusion.both_ref), custom_call_target="tpu_custom_call" | custom-call | tf_op jit(solution)/shard_map/pallas_call | solution.py:100
  513.9 3.5 copy.3
Async XLA Ops:
  6.5 101.8 %all-reduce.3.cloned.1.call-start = ((), (), s32[]{:S(2)}) async-start(), calls=%async_computation.1 | async-start | bytes 8388608 | tf_op jit(solution)/shard_map/psum | solution.py:116
  11.5 96.9 %copy-start = (f32[1024]{0:T(1024)S(1)}, f32[1024]{0:T(1024)}, u32[]{:S(2)}) copy-start(f32[1024]{0:T(1024)} %param.3) | copy-start | bytes 12292
  11.5 213.5 %all-reduce.5.cloned.1.call-start = ((), (), s32[]{:S(2)}) async-start(), calls=%async_computation.2 | async-start | bytes 8388608 | tf_op jit(solution)/shard_map/psum | solution.py:128
  120.1 229.0 %reduce-scatter.2.cloned.1.call-start = ((), (), s32[]{:S(2)}) async-start(), calls=%async_computation.3 | async-start | bytes 15728640 | tf_op jit(solution)/shard_map/reduce_scatter | solution.py:130
Sparse Core Ops, SparseCore 0:
  11.6 96.7 all-reduce.2
  120.3 104.6 all-reduce.4
  228.4 120.7 reduce-scatter.1

commit v2 on v1

--- a/solution.py
+++ b/solution.py
@@ -61,23 +61,223 @@
             work[start + STRIP :, :] = work[start + STRIP :, :] - update[start + STRIP :, :]
 
 
-def factor_kernel(both_ref, out_ref, done, work, block):
-    width, total = both_ref.shape
+def flip(index, mask_bits, log):
+    total = 0
+    for bit in range(log):
+        place = 2**bit
+        total = total + ((index // place + mask_bits // place) % 2) * place
+    return total
+
+
+def fused_kernel(
+    axes, log, real, panel_ref, design_ref, weights_ref, out_ref,
+    high_part, low_part, stage, panels, sums, landed, top, top_landed,
+    done, work, block,
+    stage_sem, panel_sem, panel_recv, panel_next, panel_pair,
+    sum_send, sum_recv, top_send, top_recv, top_arrive, top_next, top_pair, out_sem,
+):
+    n_obs, n_unk = axes
+    depth, _ = design_ref.shape
+    chunks = panels.shape[0]
+    width = chunks * BLOCK
+    rows = high_part.shape[2]
+    me = lax.axis_index("obs")
+    unk = lax.axis_index("unk")
+    odd = unk % 2
+    even = odd == 0
+    first = unk == 0
+    has_next = jnp.logical_and(even, unk + 2 < n_unk)
+    has_last = jnp.logical_and(even, unk >= 2)
+    pair = unk + 1 - 2 * odd
+    mesh_id = pl.DeviceIdType.MESH
+
+    barrier = pltpu.get_barrier_semaphore()
+
+    def greet(obs, other):
+        pl.semaphore_signal(barrier, inc=1, device_id=(obs, other), device_id_type=mesh_id)
+
+    for bit in range(log):
+        greet(flip(me, 2**bit, log), unk)
+    greet(me, pair)
+    pl.when(has_next)(lambda: greet(me, unk + 2))
+    pl.when(has_last)(lambda: greet(me, unk - 2))
+
+    def load_panel(c):
+        return pltpu.make_async_copy(
+            panel_ref.at[:, pl.ds(pl.multiple_of(c * BLOCK, BLOCK), BLOCK)],
+            panels.at[c], panel_sem.at[c],
+        )
+
+    def load_stage(piece, slot):
+        size = stage.shape[1]
+        return pltpu.make_async_copy(
+            design_ref.at[pl.ds(pl.multiple_of(piece * size, size), size), :],
+            stage.at[slot], stage_sem.at[slot],
+        )
+
+    @pl.when(first)
+    def _():
+        for c in range(chunks):
+            load_panel(c).start()
+
+    load_stage(0, 0).start()
+
+    def remote(source, target, send, recv, obs, other):
+        return pltpu.make_async_remote_copy(
+            src_ref=source, dst_ref=target, send_sem=send, recv_sem=recv,
+            device_id=(obs, other), device_id_type=mesh_id,
+        )
+
+    def panel_on(c):
+        return remote(panels.at[c], panels.at[c], panel_next.at[c], panel_recv.at[c], me, unk + 2)
+
+    def panel_across(c):
+        return remote(panels.at[c], panels.at[c], panel_pair.at[c], panel_recv.at[c], me, pair)
+
+    def top_on(c):
+        return remote(top.at[c], top.at[c], top_next.at[c], top_arrive.at[c], me, unk + 2)
+
+    def top_across(c):
+        return remote(top.at[c], top.at[c], top_pair.at[c], top_arrive.at[c], me, pair)
+
+    def forward_panel(c):
+        pl.when(has_next)(lambda: panel_on(c).start())
+        pl.when(even)(lambda: panel_across(c).start())
+
+    chained = has_next.astype(jnp.int32) + has_last.astype(jnp.int32)
+    pl.semaphore_wait(barrier, log + 1 + chained)
+
+    @pl.when(first)
+    def _():
+        def send(c, _):
+            load_panel(c).wait()
+            forward_panel(c)
+            return 0
+
+        lax.fori_loop(0, chunks, send, 0)
+
+    size = stage.shape[1]
+    pieces = depth // size
+
+    def split_piece(piece, _):
+        slot = piece % 2
+        pl.when(piece + 1 < pieces)(lambda: load_stage(piece + 1, 1 - slot).start())
+        load_stage(piece, slot).wait()
+        for owner in range(n_obs):
+            high, low = split(stage[slot, :, owner * rows : (owner + 1) * rows])
+            where = pl.ds(pl.multiple_of(piece * size, size), size)
+            high_part[owner, where, :] = high
+            low_part[owner, where, :] = low
+        return 0
+
+    lax.fori_loop(0, pieces, split_piece, 0)
+
+    def turn(level):
+        mask = (1 - odd) * 2**level + odd * 2 ** (log - 1 - level)
+        spacing = (1 - odd) * 2 ** (level + 1) + odd
+        return mask, spacing
+
+    def place(level, item):
+        return n_obs - 2 ** (log - level) + item
+
+    def sum_copy(c, level, item):
+        mask, spacing = turn(level)
+        at = place(level, item)
+        return remote(
+            sums.at[c, item * spacing + mask], landed.at[c, at],
+            sum_send.at[c, at], sum_recv.at[c, at], flip(me, mask, log), unk,
+        )
+
+    def top_copy(c, level):
+        mask, _ = turn(level)
+        return remote(
+            top.at[c], top_landed.at[c, level],
+            top_send.at[c, level], top_recv.at[c, level], flip(me, mask, log), unk,
+        )
+
+    def start_level(c, level):
+        for item in range(2 ** (log - 1 - level)):
+            sum_copy(c, level, item).start()
+        pl.when(first)(lambda: top_copy(c, level).start())
+
+    dot = functools.partial(jnp.dot, preferred_element_type=jnp.float32)
+
+    def products(c):
+        @pl.when(jnp.logical_not(first))
+        def _():
+            panel_across(c).wait_recv()
+            forward_panel(c)
+
+        weighted = jnp.transpose(panels[c] * weights_ref[...])
+        high, low = split(weighted)
+        both = jnp.concatenate([high, low], axis=0)
+
+        def owner_block(q, _):
+            owner = flip(me, q, log)
+            wide = dot(both, high_part[owner])
+            sums[c, q] = wide[:BLOCK] + wide[BLOCK:] + dot(high, low_part[owner])
+            return 0
+
+        lax.fori_loop(0, n_obs, owner_block, 0)
+
+        @pl.when(first)
+        def _():
+            for owner in range(n_obs):
+                start, stop = owner * real, min((owner + 1) * real, width)
+                if start < stop:
+                    top[c, :, start:stop] = sums[c, flip(me, owner, log), :, : stop - start]
+
+        start_level(c, 0)
+
+    def reduce_level(c, level):
+        _, spacing = turn(level)
+        for item in range(2 ** (log - 1 - level)):
+            sum_copy(c, level, item).wait_recv()
+            here = item * spacing
+            sums[c, here] = sums[c, here] + landed[c, place(level, item)]
+
+        @pl.when(first)
+        def _():
+            top_copy(c, level).wait()
+            top[c] = top[c] + top_landed[c, level]
+
+        if level + 1 < log:
+            start_level(c, level + 1)
+        else:
+            @pl.when(first)
+            def _():
+                pl.when(has_next)(lambda: top_on(c).start())
+                top_across(c).start()
+
     eye = (
         lax.broadcasted_iota(jnp.int32, (BLOCK, BLOCK), 0)
         == lax.broadcasted_iota(jnp.int32, (BLOCK, BLOCK), 1)
     ).astype(jnp.float32)
 
-    def step(k, _):
+    def out_copy(c):
+        return pltpu.make_async_copy(
+            sums.at[c, 0],
+            out_ref.at[pl.ds(pl.multiple_of(c * BLOCK, BLOCK), BLOCK), :],
+            out_sem.at[c],
+        )
+
+    def factor(k):
+        @pl.when(jnp.logical_not(first))
+        def _():
+            top_across(k).wait_recv()
+            pl.when(has_next)(lambda: top_on(k).start())
+            pl.when(even)(lambda: top_across(k).start())
+
         offset = pl.multiple_of(k * BLOCK, BLOCK)
-        block[...] = both_ref[pl.ds(offset, BLOCK), :]
+        block[:, :width] = top[k]
+        block[:, width:] = sums[k, 0]
 
         def earlier(j, _):
             held = done[j, :, pl.ds(offset, BLOCK)]
-            left = jnp.concatenate(
-                [held[:BLOCK], held[2 * BLOCK :], held[BLOCK : 2 * BLOCK]], axis=0
+            swapped = jnp.concatenate([held[BLOCK:], held[:BLOCK]], axis=0)
+            block[...] = block[...] - (
+                dot_t(swapped, done[j]) + dot_t(held[:BLOCK], done[j, :BLOCK, :])
             )
-            block[...] = block[...] - dot_t(left, done[j])
             return 0
 
         lax.fori_loop(0, k, earlier, 0)
@@ -87,53 +287,99 @@
         column = dot_3(work[:, BLOCK:], block[...])
         high, low = split(column)
         done[k, :BLOCK, :] = high
-        done[k, BLOCK : 2 * BLOCK, :] = low
-        done[k, 2 * BLOCK :, :] = high
-        out_ref[pl.ds(offset, BLOCK), :] = column[:, width:]
+        done[k, BLOCK:, :] = low
+        sums[k, 0] = column[:, width:]
+        out_copy(k).start()
+
+    def step(t, _):
+        pl.when(t < chunks)(lambda: products(t))
+        for level in range(log):
+            c = t - 1 - level
+            pl.when(jnp.logical_and(c >= 0, c < chunks))(functools.partial(reduce_level, c, level))
+        pl.when(t >= log + 1)(lambda: factor(t - log - 1))
         return 0
 
-    lax.fori_loop(0, width // BLOCK, step, 0)
-
-
-def factor_rows(both):
-    width, total = both.shape
+    lax.fori_loop(0, chunks + log + 1, step, 0)
+
+    def drain(c, _):
+        out_copy(c).wait()
+        for level in range(log):
+            for item in range(2 ** (log - 1 - level)):
+                sum_copy(c, level, item).wait_send()
+
+        @pl.when(has_next)
+        def _():
+            panel_on(c).wait_send()
+            top_on(c).wait_send()
+
+        @pl.when(even)
+        def _():
+            panel_across(c).wait_send()
+            top_across(c).wait_send()
+
+        return 0
+
+    lax.fori_loop(0, chunks, drain, 0)
+
+
+def fused(axes, real, panel, design, weights):
+    n_obs, n_unk = axes
+    log = n_obs.bit_length() - 1
+    depth, columns = design.shape
+    rows = columns // n_obs
+    width = 2 * PANEL
+    chunks = width // BLOCK
+    piece = 64
+    f32, bf16, dma = jnp.float32, jnp.bfloat16, pltpu.SemaphoreType.DMA
     return pl.pallas_call(
-        factor_kernel,
-        out_shape=jax.ShapeDtypeStruct((width, total - width), jnp.float32),
-        in_specs=[pl.BlockSpec(memory_space=pltpu.VMEM)],
-        out_specs=pl.BlockSpec(memory_space=pltpu.VMEM),
+        functools.partial(fused_kernel, axes, log, real),
+        out_shape=jax.ShapeDtypeStruct((width, rows), f32),
+        in_specs=[
+            pl.BlockSpec(memory_space=pl.ANY),
+            pl.BlockSpec(memory_space=pl.ANY),
+            pl.BlockSpec(memory_space=pltpu.VMEM),
+        ],
+        out_specs=pl.BlockSpec(memory_space=pl.ANY),
         scratch_shapes=[
-            pltpu.VMEM((width // BLOCK, 3 * BLOCK, total), jnp.bfloat16),
-            pltpu.VMEM((BLOCK, 2 * BLOCK), jnp.float32),
-            pltpu.VMEM((BLOCK, total), jnp.float32),
+            pltpu.VMEM((n_obs, depth, rows), bf16),
+            pltpu.VMEM((n_obs, depth, rows), bf16),
+            pltpu.VMEM((2, piece, columns), f32),
+            pltpu.VMEM((chunks, depth, BLOCK), f32),
+            pltpu.VMEM((chunks, n_obs, BLOCK, rows), f32),
+            pltpu.VMEM((chunks, n_obs - 1, BLOCK, rows), f32),
+            pltpu.VMEM((chunks, BLOCK, width), f32),
+            pltpu.VMEM((chunks, log, BLOCK, width), f32),
+            pltpu.VMEM((chunks, 2 * BLOCK, width + rows), bf16),
+            pltpu.VMEM((BLOCK, 2 * BLOCK), f32),
+            pltpu.VMEM((BLOCK, width + rows), f32),
+            dma((2,)), dma((chunks,)), dma((chunks,)), dma((chunks,)), dma((chunks,)),
+            dma((chunks, n_obs - 1)), dma((chunks, n_obs - 1)),
+            dma((chunks, log)), dma((chunks, log)),
+            dma((chunks,)), dma((chunks,)), dma((chunks,)), dma((chunks,)),
         ],
-        compiler_params=pltpu.CompilerParams(vmem_limit_bytes=56 * 2**20),
-    )(both)
-
-
-def spread(block, axis, holder):
-    block = jnp.where(lax.axis_index(axis) == holder, block, jnp.zeros_like(block))
-    return lax.psum(block, axis)
-
-
-def local(design, weights):
-    panel_cols = spread(design[:, : 2 * PANEL], "unk", 0)
-    weighted = panel_cols * weights[:, None]
-    dot = functools.partial(
-        lax.dot_general,
-        dimension_numbers=(((0,), (0,)), ((), ())),
-        precision=lax.Precision.HIGH,
-        preferred_element_type=jnp.float32,
-    )
-    top_block = lax.psum(dot(weighted, panel_cols), "obs")
-    partial_value = dot(weighted, design)
-    owned = lax.psum_scatter(partial_value, "obs", scatter_dimension=1, tiled=True)
-    return factor_rows(jnp.concatenate([top_block, owned], axis=1)).T
+        compiler_params=pltpu.CompilerParams(
+            collective_id=0, has_side_effects=True, vmem_limit_bytes=64 * 2**20 - 2**16
+        ),
+    )(panel, design, weights)
+
+
+def local(axes, design, weights):
+    n_obs, _ = axes
+    depth, columns = design.shape
+    rows = columns // n_obs
+    padded = -(-rows // BLOCK) * BLOCK
+    panel = design
+    if padded != rows:
+        design = jnp.pad(
+            design.reshape(depth, n_obs, rows), ((0, 0), (0, 0), (0, padded - rows))
+        ).reshape(depth, n_obs * padded)
+    return fused(axes, rows, panel, design, weights[:, None])[:, :rows].T
 
 
 def solution(mesh):
+    axes = (mesh.shape["obs"], mesh.shape["unk"])
     return jax.shard_map(
-        local,
+        functools.partial(local, axes),
         mesh=mesh,
         in_specs=(P("obs", "unk"), P("obs")),
         out_specs=P(("unk", "obs"), None),

time: 526 us -> 266 us (0.51)
  waiting for transfers between devices: 297 us -> 0 us
  Pallas kernels: 158 us -> 261 us
  matrix products: 40.4 us -> 0 us
  between operations: 13.1 us -> 0.01 us
  other arithmetic: 11.6 us -> 0 us
    psum x2 -> x0, waiting for transfers between devices: 173 us -> none  [the longest x1 96.8 us: spread(): return lax.psum(block, axis)]
    reduce_scatter x1 -> x0, waiting for transfers between devices: 124 us -> none  [local(): lax.psum_scatter(partial_value, 'obs', scatter_dimension=1, tiled=True)]
    pallas_call x1, Pallas kernels: 158 us -> 261 us  [fused(): pl.pallas_call(functools.partial(fused_kernel, axes, log, real), out_shap...]
    dot_general x2 -> x0, matrix products: 40.4 us -> none  [the longest x1 28.7 us: local(): partial_value = dot(weighted, design)]
    concatenate x1 -> x0, other arithmetic: 6.67 us -> none  [local(): return factor_rows(jnp.concatenate([top_block, owned], axis=1)).T]
  transfers between devices with their start and end apart: 3 -> 0, of which waited for: 3 -> 0; matrix products, arithmetic and copies ran while one was open for 5% -> 0% of each run, Pallas kernels for 0% -> 0%
where the time goes in v2:
time: 266 us
  Pallas kernels  261 us (98%)
  local copies, waits for them, and re-layouts  5.25 us (2%)
    pallas_call x1, Pallas kernels, fused(): pl.pallas_call(functools.partial(fused_kernel, axes, log, real), out_shap...  261 us

profile of v2, /device:TPU:25, one launch (start us, length us, event | category | flops | bytes accessed | tf_op | source)
XLA Modules:
  0.0 266.0 jit_solution(5874925300432892916)
XLA Ops:
  0.0 1.7 copy.4.weights_ref
  1.7 260.7 %shard_map.28 = f32[1024,768]{1,0:T(8,128)} custom-call(f32[1024,3072]{1,0:T(8,128)} %design_ref.1, f32[1024,3072]{1,0:T(8,128)} %design_ref.1, f32[1024,1]{1,0:T(8,128)} %copy.4.weights_ref), custom_call_target="tpu_custom_call" | custom-call | tf_op jit(solution)/shard_map/pallas_call | solution.py:334
  262.4 3.5 %copy.5 = f32[768,1024]{1,0:T(8,128)} copy(f32[768,1024]{0,1:T(8,128)} %bitcast.2) | data formatting | bytes 6291456 | tf_op jit(solution)/shard_map/transpose | solution.py:376

commit v3 on v2

--- a/solution.py
+++ b/solution.py
@@ -8,7 +8,7 @@
 
 PANEL = 512
 BLOCK = 128
-STRIP = 8
+STRIP = 16
 
 
 def split(value):
@@ -30,34 +30,66 @@
     return dot(left_high, right_high) + dot(left_high, right_low) + dot(left_low, right_high)
 
 
+def spread_row(value, index):
+    return jnp.broadcast_to(value[index : index + 1, :], value.shape)
+
+
 def invert_factor(work):
-    row = lax.broadcasted_iota(jnp.int32, (STRIP, 2 * BLOCK), 0)
+    half = STRIP // 2
+    row = lax.broadcasted_iota(jnp.int32, (half, BLOCK), 0)
     for strip in range(BLOCK // STRIP):
         start = strip * STRIP
-        rows = work[start : start + STRIP, :]
-        scale = jnp.zeros_like(rows)
-        for step in range(STRIP):
-            column = jnp.broadcast_to(
-                rows[:, start + step : start + step + 1], (STRIP, 2 * BLOCK)
+        upper = work[start : start + half, :]
+        lower = work[start + half : start + STRIP, :]
+
+        def lanes(value, index):
+            return jnp.broadcast_to(
+                value[:, start + index : start + index + 1], (half, BLOCK)
             )
-            pivot = jnp.broadcast_to(column[step : step + 1, :], (STRIP, 2 * BLOCK))
-            scale = jnp.where(row == step, pivot, scale)
-            if step < STRIP - 1:
-                pivot_row = jnp.broadcast_to(rows[step : step + 1, :], (STRIP, 2 * BLOCK))
-                factor = jnp.where(row > step, column / pivot, 0.0)
-                rows = rows - factor * pivot_row
-        rows = rows * lax.rsqrt(scale)
+
+        columns_up = [lanes(upper, index) for index in range(STRIP)]
+        columns_down = [lanes(lower, index) for index in range(STRIP)]
+        rest_up = [upper[:, :BLOCK], upper[:, BLOCK:]]
+        rest_down = [lower[:, :BLOCK], lower[:, BLOCK:]]
+        scale_up = jnp.zeros((half, BLOCK), jnp.float32)
+        scale_down = scale_up
+        for step in range(half):
+            pivot = spread_row(columns_up[step], step)
+            scale_up = jnp.where(row == step, pivot, scale_up)
+            inverse = 1.0 / pivot
+            factor_up = jnp.where(row > step, columns_up[step] * inverse, 0.0)
+            factor_down = columns_down[step] * inverse
+            for up, down in ((columns_up, columns_down), (rest_up, rest_down)):
+                for index in range(step + 1 if up is columns_up else 0, len(up)):
+                    pivot_row = spread_row(up[index], step)
+                    up[index] = up[index] - factor_up * pivot_row
+                    down[index] = down[index] - factor_down * pivot_row
+        for step in range(half):
+            pivot = spread_row(columns_down[half + step], step)
+            scale_down = jnp.where(row == step, pivot, scale_down)
+            if step < half - 1:
+                inverse = 1.0 / pivot
+                factor_down = jnp.where(row > step, columns_down[half + step] * inverse, 0.0)
+                for down, begin in ((columns_down, half + step + 1), (rest_down, 0)):
+                    for index in range(begin, len(down)):
+                        down[index] = down[index] - factor_down * spread_row(down[index], step)
+        root_up, root_down = lax.rsqrt(scale_up), lax.rsqrt(scale_down)
+        rows = jnp.concatenate(
+            [
+                jnp.concatenate([value * root_up for value in rest_up], axis=1),
+                jnp.concatenate([value * root_down for value in rest_down], axis=1),
+            ],
+            axis=0,
+        )
         work[start : start + STRIP, :] = rows
         if start + STRIP < BLOCK:
-            first = rows.astype(jnp.bfloat16).astype(jnp.float32)
-            rest = rows - first
-            second = rest.astype(jnp.bfloat16).astype(jnp.float32)
-            third = rest - second
+            first = rows.astype(jnp.bfloat16)
+            rest = rows - first.astype(jnp.float32)
+            second = rest.astype(jnp.bfloat16)
+            third = (rest - second.astype(jnp.float32)).astype(jnp.bfloat16)
             right = jnp.concatenate([first, second, first, second, third, first], axis=0)
             left = jnp.concatenate([first, first, second, second, first, third], axis=0)
-            update = dot_t(
-                left[:, :BLOCK].astype(jnp.bfloat16), right.astype(jnp.bfloat16)
-            )
+            update = dot_t(left[:, :BLOCK], right)
             work[start + STRIP :, :] = work[start + STRIP :, :] - update[start + STRIP :, :]
 
 

time: 266 us -> 219 us (0.82)
  Pallas kernels: 261 us -> 213 us
    pallas_call x1, Pallas kernels: 261 us -> 213 us  [fused(): pl.pallas_call(functools.partial(fused_kernel, axes, log, real), out_shap...]
where the time goes in v3:
time: 219 us
  Pallas kernels  213 us (97%)
  local copies, waits for them, and re-layouts  5.25 us (2%)
    pallas_call x1, Pallas kernels, fused(): pl.pallas_call(functools.partial(fused_kernel, axes, log, real), out_shap...  213 us

profile of v3, /device:TPU:25, one launch (start us, length us, event | category | flops | bytes accessed | tf_op | source)
XLA Modules:
  0.0 218.7 jit_solution(5267623339646721156)
XLA Ops:
  0.0 1.7 copy.4.weights_ref
  1.7 213.5 %shard_map.28 = f32[1024,768]{1,0:T(8,128)} custom-call(f32[1024,3072]{1,0:T(8,128)} %design_ref.1, f32[1024,3072]{1,0:T(8,128)} %design_ref.1, f32[1024,1]{1,0:T(8,128)} %copy.4.weights_ref), custom_call_target="tpu_custom_call" | custom-call | tf_op jit(solution)/shard_map/pallas_call | solution.py:366
  215.2 3.5 %copy.5 = f32[768,1024]{1,0:T(8,128)} copy(f32[768,1024]{0,1:T(8,128)} %bitcast.2) | data formatting | bytes 6291456 | tf_op jit(solution)/shard_map/transpose | solution.py:408

commit v4 on v3

--- a/solution.py
+++ b/solution.py
@@ -9,6 +9,7 @@
 PANEL = 512
 BLOCK = 128
 STRIP = 16
+GROUP = 2
 
 
 def split(value):
@@ -166,11 +167,21 @@
     def panel_across(c):
         return remote(panels.at[c], panels.at[c], panel_pair.at[c], panel_recv.at[c], me, pair)
 
-    def top_on(c):
-        return remote(top.at[c], top.at[c], top_next.at[c], top_arrive.at[c], me, unk + 2)
-
-    def top_across(c):
-        return remote(top.at[c], top.at[c], top_pair.at[c], top_arrive.at[c], me, pair)
+    def in_group(c, action):
+        for group in range(chunks // GROUP):
+            pl.when(c // GROUP == group)(functools.partial(action, group * GROUP * BLOCK))
+
+    def top_on(c, begin):
+        part = top.at[c, :, begin:]
+        return remote(part, part, top_next.at[c], top_arrive.at[c], me, unk + 2)
+
+    def top_across(c, begin):
+        part = top.at[c, :, begin:]
+        return remote(part, part, top_pair.at[c], top_arrive.at[c], me, pair)
+
+    def forward_top(c, begin):
+        pl.when(has_next)(lambda: top_on(c, begin).start())
+        pl.when(even)(lambda: top_across(c, begin).start())
 
     def forward_panel(c):
         pl.when(has_next)(lambda: panel_on(c).start())
@@ -220,17 +231,17 @@
             sum_send.at[c, at], sum_recv.at[c, at], flip(me, mask, log), unk,
         )
 
-    def top_copy(c, level):
+    def top_copy(c, level, begin):
         mask, _ = turn(level)
         return remote(
-            top.at[c], top_landed.at[c, level],
+            top.at[c, :, begin:], top_landed.at[c, level, :, begin:],
             top_send.at[c, level], top_recv.at[c, level], flip(me, mask, log), unk,
         )
 
     def start_level(c, level):
         for item in range(2 ** (log - 1 - level)):
             sum_copy(c, level, item).start()
-        pl.when(first)(lambda: top_copy(c, level).start())
+        pl.when(first)(lambda: in_group(c, lambda begin: top_copy(c, level, begin).start()))
 
     dot = functools.partial(jnp.dot, preferred_element_type=jnp.float32)
 
@@ -240,7 +251,7 @@
             panel_across(c).wait_recv()
             forward_panel(c)
 
-        weighted = jnp.transpose(panels[c] * weights_ref[...])
+        weighted = jnp.transpose(panels[c]) * weights_ref[...]
         high, low = split(weighted)
         both = jnp.concatenate([high, low], axis=0)
 
@@ -270,16 +281,16 @@
 
         @pl.when(first)
         def _():
-            top_copy(c, level).wait()
-            top[c] = top[c] + top_landed[c, level]
+            def add(begin):
+                top_copy(c, level, begin).wait()
+                top[c, :, begin:] = top[c, :, begin:] + top_landed[c, level, :, begin:]
+
+            in_group(c, add)
 
         if level + 1 < log:
             start_level(c, level + 1)
         else:
-            @pl.when(first)
-            def _():
-                pl.when(has_next)(lambda: top_on(c).start())
-                top_across(c).start()
+            pl.when(first)(lambda: in_group(c, functools.partial(forward_top, c)))
 
     eye = (
         lax.broadcasted_iota(jnp.int32, (BLOCK, BLOCK), 0)
@@ -296,31 +307,42 @@
     def factor(k):
         @pl.when(jnp.logical_not(first))
         def _():
-            top_across(k).wait_recv()
-            pl.when(has_next)(lambda: top_on(k).start())
-            pl.when(even)(lambda: top_across(k).start())
+            def arrive(begin):
+                top_across(k, begin).wait_recv()
+                forward_top(k, begin)
+
+            in_group(k, arrive)
 
         offset = pl.multiple_of(k * BLOCK, BLOCK)
-        block[:, :width] = top[k]
-        block[:, width:] = sums[k, 0]
-
-        def earlier(j, _):
-            held = done[j, :, pl.ds(offset, BLOCK)]
-            swapped = jnp.concatenate([held[BLOCK:], held[:BLOCK]], axis=0)
-            block[...] = block[...] - (
-                dot_t(swapped, done[j]) + dot_t(held[:BLOCK], done[j, :BLOCK, :])
-            )
-            return 0
-
-        lax.fori_loop(0, k, earlier, 0)
+
+        def update(begin):
+            block[:, begin:width] = top[k, :, begin:]
+            block[:, width:] = sums[k, 0]
+
+            def earlier(j, _):
+                held = done[j, :, pl.ds(offset, BLOCK)]
+                swapped = jnp.concatenate([held[BLOCK:], held[:BLOCK]], axis=0)
+                block[:, begin:] = block[:, begin:] - (
+                    dot_t(swapped, done[j, :, begin:])
+                    + dot_t(held[:BLOCK], done[j, :BLOCK, begin:])
+                )
+                return 0
+
+            lax.fori_loop(0, k, earlier, 0)
+
+        in_group(k, update)
         work[:, :BLOCK] = block[:, pl.ds(offset, BLOCK)]
         work[:, BLOCK:] = eye
         invert_factor(work)
-        column = dot_3(work[:, BLOCK:], block[...])
-        high, low = split(column)
-        done[k, :BLOCK, :] = high
-        done[k, BLOCK:, :] = low
-        sums[k, 0] = column[:, width:]
+
+        def solve(begin):
+            column = dot_3(work[:, BLOCK:], block[:, begin:])
+            high, low = split(column)
+            done[k, :BLOCK, begin:] = high
+            done[k, BLOCK:, begin:] = low
+            sums[k, 0] = column[:, width - begin :]
+
+        in_group(k, solve)
         out_copy(k).start()
 
     def step(t, _):
@@ -328,10 +350,10 @@
         for level in range(log):
             c = t - 1 - level
             pl.when(jnp.logical_and(c >= 0, c < chunks))(functools.partial(reduce_level, c, level))
-        pl.when(t >= log + 1)(lambda: factor(t - log - 1))
+        pl.when(t >= log)(lambda: factor(t - log))
         return 0
 
-    lax.fori_loop(0, chunks + log + 1, step, 0)
+    lax.fori_loop(0, chunks + log, step, 0)
 
     def drain(c, _):
         out_copy(c).wait()
@@ -342,12 +364,12 @@
         @pl.when(has_next)
         def _():
             panel_on(c).wait_send()
-            top_on(c).wait_send()
+            in_group(c, lambda begin: top_on(c, begin).wait_send())
 
         @pl.when(even)
         def _():
             panel_across(c).wait_send()
-            top_across(c).wait_send()
+            in_group(c, lambda begin: top_across(c, begin).wait_send())
 
         return 0
 
@@ -405,7 +427,7 @@
         design = jnp.pad(
             design.reshape(depth, n_obs, rows), ((0, 0), (0, 0), (0, padded - rows))
         ).reshape(depth, n_obs * padded)
-    return fused(axes, rows, panel, design, weights[:, None])[:, :rows].T
+    return fused(axes, rows, panel, design, weights[None, :])[:, :rows].T
 
 
 def solution(mesh):

time: 219 us -> 183 us (0.84)
  Pallas kernels: 213 us -> 178 us
    pallas_call x1, Pallas kernels: 213 us -> 178 us  [fused(): pl.pallas_call(functools.partial(fused_kernel, axes, log, real), out_shap...]
where the time goes in v4:
time: 183 us; the launch traced here: 182 us
  Pallas kernels  178 us (97%)
  local copies, waits for them, and re-layouts  3.55 us (2%)
    pallas_call x1, Pallas kernels, fused(): pl.pallas_call(functools.partial(fused_kernel, axes, log, real), out_shap...  178 us

profile of v4, /device:TPU:25, one launch (start us, length us, event | category | flops | bytes accessed | tf_op | source)
XLA Modules:
  0.0 181.9 jit_solution(16980351901657727283)
XLA Ops:
  0.0 178.4 %shard_map.28 = f32[1024,768]{1,0:T(8,128)} custom-call(f32[1024,3072]{1,0:T(8,128)} %design_ref.1, f32[1024,3072]{1,0:T(8,128)} %design_ref.1, f32[1,1024]{1,0:T(1,128)} %bitcast.3), custom_call_target="tpu_custom_call" | custom-call | tf_op jit(solution)/shard_map/pallas_call | solution.py:388
  178.4 3.5 %copy.3 = f32[768,1024]{1,0:T(8,128)} copy(f32[768,1024]{0,1:T(8,128)} %bitcast.2) | data formatting | bytes 6291456 | tf_op jit(solution)/shard_map/transpose | solution.py:430

commit v5 on v4

--- a/solution.py
+++ b/solution.py
@@ -10,6 +10,7 @@
 BLOCK = 128
 STRIP = 16
 GROUP = 2
+PARTS = 4
 
 
 def split(value):
@@ -161,11 +162,15 @@
             device_id=(obs, other), device_id_type=mesh_id,
         )
 
-    def panel_on(c):
-        return remote(panels.at[c], panels.at[c], panel_next.at[c], panel_recv.at[c], me, unk + 2)
-
-    def panel_across(c):
-        return remote(panels.at[c], panels.at[c], panel_pair.at[c], panel_recv.at[c], me, pair)
+    part_rows = depth // PARTS
+
+    def panel_on(c, h):
+        part = panels.at[c, h * part_rows : (h + 1) * part_rows, :]
+        return remote(part, part, panel_next.at[c, h], panel_recv.at[c, h], me, unk + 2)
+
+    def panel_across(c, h):
+        part = panels.at[c, h * part_rows : (h + 1) * part_rows, :]
+        return remote(part, part, panel_pair.at[c, h], panel_recv.at[c, h], me, pair)
 
     def in_group(c, action):
         for group in range(chunks // GROUP):
@@ -183,9 +188,14 @@
         pl.when(has_next)(lambda: top_on(c, begin).start())
         pl.when(even)(lambda: top_across(c, begin).start())
 
-    def forward_panel(c):
-        pl.when(has_next)(lambda: panel_on(c).start())
-        pl.when(even)(lambda: panel_across(c).start())
+    def forward_panel(c, h):
+        pl.when(has_next)(lambda: panel_on(c, h).start())
+        pl.when(even)(lambda: panel_across(c, h).start())
+
+    def take_panel(c):
+        for h in range(PARTS):
+            panel_across(c, h).wait_recv()
+            forward_panel(c, h)
 
     chained = has_next.astype(jnp.int32) + has_last.astype(jnp.int32)
     pl.semaphore_wait(barrier, log + 1 + chained)
@@ -194,7 +204,8 @@
     def _():
         def send(c, _):
             load_panel(c).wait()
-            forward_panel(c)
+            for h in range(PARTS):
+                forward_panel(c, h)
             return 0
 
         lax.fori_loop(0, chunks, send, 0)
@@ -213,7 +224,10 @@
             low_part[owner, where, :] = low
         return 0
 
-    lax.fori_loop(0, pieces, split_piece, 0)
+    passes_on = jnp.logical_and(has_next, jnp.logical_not(first))
+    lax.fori_loop(0, pieces // 2, split_piece, 0)
+    pl.when(passes_on)(lambda: take_panel(0))
+    lax.fori_loop(pieces // 2, pieces, split_piece, 0)
 
     def turn(level):
         mask = (1 - odd) * 2**level + odd * 2 ** (log - 1 - level)
@@ -246,11 +260,8 @@
     dot = functools.partial(jnp.dot, preferred_element_type=jnp.float32)
 
     def products(c):
-        @pl.when(jnp.logical_not(first))
-        def _():
-            panel_across(c).wait_recv()
-            forward_panel(c)
-
+        taken = jnp.logical_or(first, jnp.logical_and(passes_on, c == 0))
+        pl.when(jnp.logical_not(taken))(lambda: take_panel(c))
         weighted = jnp.transpose(panels[c]) * weights_ref[...]
         high, low = split(weighted)
         both = jnp.concatenate([high, low], axis=0)
@@ -363,12 +374,14 @@
 
         @pl.when(has_next)
         def _():
-            panel_on(c).wait_send()
+            for h in range(PARTS):
+                panel_on(c, h).wait_send()
             in_group(c, lambda begin: top_on(c, begin).wait_send())
 
         @pl.when(even)
         def _():
-            panel_across(c).wait_send()
+            for h in range(PARTS):
+                panel_across(c, h).wait_send()
             in_group(c, lambda begin: top_across(c, begin).wait_send())
 
         return 0
@@ -406,7 +419,8 @@
             pltpu.VMEM((chunks, 2 * BLOCK, width + rows), bf16),
             pltpu.VMEM((BLOCK, 2 * BLOCK), f32),
             pltpu.VMEM((BLOCK, width + rows), f32),
-            dma((2,)), dma((chunks,)), dma((chunks,)), dma((chunks,)), dma((chunks,)),
+            dma((2,)), dma((chunks,)),
+            dma((chunks, PARTS)), dma((chunks, PARTS)), dma((chunks, PARTS)),
             dma((chunks, n_obs - 1)), dma((chunks, n_obs - 1)),
             dma((chunks, log)), dma((chunks, log)),
             dma((chunks,)), dma((chunks,)), dma((chunks,)), dma((chunks,)),

time: 183 us -> 182 us (level)
  no operation moved by 1% of the time
where the time goes in v5:
time: 182 us; the launch traced here: 181 us
  Pallas kernels  178 us (98%)
  local copies, waits for them, and re-layouts  3.55 us (2%)
    pallas_call x1, Pallas kernels, fused(): pl.pallas_call(functools.partial(fused_kernel, axes, log, real), out_shap...  178 us

profile of v5, /device:TPU:25, one launch (start us, length us, event | category | flops | bytes accessed | tf_op | source)
XLA Modules:
  0.0 181.4 jit_solution(12932398761574274489)
XLA Ops:
  0.0 177.9 %shard_map.28 = f32[1024,768]{1,0:T(8,128)} custom-call(f32[1024,3072]{1,0:T(8,128)} %design_ref.1, f32[1024,3072]{1,0:T(8,128)} %design_ref.1, f32[1,1024]{1,0:T(1,128)} %bitcast.3), custom_call_target="tpu_custom_call" | custom-call | tf_op jit(solution)/shard_map/pallas_call | solution.py:401
  177.9 3.5 %copy.3 = f32[768,1024]{1,0:T(8,128)} copy(f32[768,1024]{0,1:T(8,128)} %bitcast.2) | data formatting | bytes 6291456 | tf_op jit(solution)/shard_map/transpose | solution.py:444
